TPU v7x, 32 devices: a whole 2x2x4 slice. The times are simulated.
32 devices in a mesh: row: 4 (over z), col: 8 (over y, x, core).
Axes of the slice: x: 2, y: 2, z: 4, core: 2. Of those that a mesh axis runs over, the one named last changes fastest.
Arguments:
- tokens: bfloat16 [1024, 2048], P(('row', 'col')), may hold values from -6 to 6
- routes: int32 [1024, 6], P(('row', 'col')), may hold values from 0 to 63, as said below
- router: bfloat16 [2048, 64], replicated, may hold values from -0.125 to 0.125
- w_in: bfloat16 [128, 2048, 1408], P(('row', 'col')), may hold values from -0.125 to 0.125
- w_out: bfloat16 [128, 704, 2048], P(('row', 'col')), may hold values from -0.15625 to 0.15625
- cache_prefill: bfloat16 [2304, 9216], P(('row', 'col')), may hold values from -6 to 6
- page_slot: int32 [2304], P(('row', 'col')), may hold values from 0 to 2303, as said below
Outputs:
- moe_out: bfloat16 [1024, 2048], P(('row', 'col'))
- cache_decode: bfloat16 [2304, 9216], P(('row', 'col'))
Inputs may be any that keep to these rules, and one draw needn't show every extreme that they name: `routes`: each row names 6 different experts. In the rows of one device no expert is named more than 6 times, and one expert, the same for all devices, is named exactly 6 times in every device's rows. `page_slot`: A permutation of the page rows. Every device receives exactly 72 pages; at most 3 pages go from one device to one device, and some pair of devices reaches 3.
All inputs are finite; a program needn't handle non-finite values.
Results may differ from a plain program's by a relative error of at most 0.0065.
Values may be sent and summed in bfloat16 or wider, within the bound.
A program may use at most 128 MiB of HBM per device.

v0:
```python
import jax
import jax.numpy as jnp
from jax import lax
from jax.sharding import PartitionSpec as P

EXPERTS = 64
CAPE = 6


route_scale = 2.446


def gate_values_of(tokens, routes, router):
    logits = jnp.dot(tokens, router, preferred_element_type=jnp.float32)
    scores = jax.nn.sigmoid(logits)
    picked = jnp.take_along_axis(scores, routes, axis=1)
    return route_scale * picked / jnp.sum(picked, axis=1, keepdims=True)


def expert_halves(buffer, w_in, w_out):
    gate_up = jnp.einsum("ajcd,jdf->ajcf", buffer, w_in, preferred_element_type=jnp.float32)
    hidden_width = w_out.shape[1]
    activated = (jax.nn.silu(gate_up[..., :hidden_width]) * gate_up[..., hidden_width:]).astype(
        jnp.bfloat16
    )
    return jnp.einsum(
        "ajcf,jfd->ajcd", activated, w_out, preferred_element_type=jnp.float32
    ).astype(jnp.bfloat16)


def move_pages(cache_prefill, page_slot):
    devices = lax.axis_size("row") * lax.axis_size("col")
    pages_here, page_width = cache_prefill.shape
    page_cap = pages_here // devices + 1
    target = page_slot // pages_here
    within = page_slot % pages_here
    onehot_dest = (target[:, None] == jnp.arange(devices, dtype=jnp.int32)[None, :]).astype(
        jnp.int32
    )
    before = jnp.cumsum(onehot_dest, axis=0) - onehot_dest
    ranking = jnp.sum(before * onehot_dest, axis=1)
    placed = target * page_cap + ranking
    source_of = (
        jnp.full((devices * page_cap,), pages_here, jnp.int32)
        .at[placed]
        .set(jnp.arange(pages_here, dtype=jnp.int32))
    )
    landing = jnp.full((devices * page_cap,), pages_here, jnp.int32).at[placed].set(within)
    extended = jnp.concatenate(
        [cache_prefill, jnp.zeros((1, page_width), cache_prefill.dtype)], axis=0
    )
    outgoing = extended[source_of].reshape(devices, page_cap, page_width)
    arrived, arrived_slot = (
        lax.all_to_all(outgoing, ("row", "col"), split_axis=0, concat_axis=0, tiled=True),
        lax.all_to_all(
            landing.reshape(devices, page_cap),
            ("row", "col"),
            split_axis=0,
            concat_axis=0,
            tiled=True,
        ),
    )
    placed_rows = (
        jnp.zeros_like(extended).at[arrived_slot.reshape(-1)].set(arrived.reshape(-1, page_width))
    )
    return placed_rows[:pages_here]


def per_device(tokens, routes, router, w_in, w_out, cache_prefill, page_slot):
    cache_decode = move_pages(cache_prefill, page_slot)
    devices = lax.axis_size("row") * lax.axis_size("col")
    tok_count, model_width = tokens.shape
    top_count = routes.shape[1]
    halves_here = w_in.shape[0]
    gate_values = gate_values_of(tokens, routes, router)
    flat_routes = routes.reshape(-1)
    onehot_expert = (flat_routes[:, None] == jnp.arange(EXPERTS, dtype=jnp.int32)[None, :]).astype(
        jnp.int32
    )
    ranking = jnp.sum((jnp.cumsum(onehot_expert, axis=0) - onehot_expert) * onehot_expert, axis=1)
    slot_index = flat_routes * CAPE + ranking
    token_of = jnp.arange(tok_count * top_count, dtype=jnp.int32) // top_count
    slot_token = jnp.full((EXPERTS * CAPE,), tok_count, jnp.int32).at[slot_index].set(token_of)
    extended = jnp.concatenate([tokens, jnp.zeros((1, model_width), tokens.dtype)], axis=0)
    slot_rows = extended[slot_token]
    outgoing = jnp.broadcast_to(slot_rows[None], (2,) + slot_rows.shape)
    outgoing = outgoing.reshape(devices, halves_here, CAPE, model_width)
    returned = lax.all_to_all(
        expert_halves(
            lax.all_to_all(outgoing, ("row", "col"), split_axis=0, concat_axis=0, tiled=True),
            w_in,
            w_out,
        ),
        ("row", "col"),
        split_axis=0,
        concat_axis=0,
        tiled=True,
    )
    returned = returned.reshape(2, EXPERTS * CAPE, model_width)
    expert_out = (returned[0].astype(jnp.float32) + returned[1].astype(jnp.float32)).astype(
        jnp.bfloat16
    )
    picked_out = (
        expert_out[slot_index].reshape(tok_count, top_count, model_width).astype(jnp.float32)
    )
    moe_out = jnp.sum(picked_out * gate_values[:, :, None], axis=1).astype(jnp.bfloat16)
    return (moe_out, cache_decode)


def solution(mesh):
    in_specs = (
        P(("row", "col"), None),
        P(("row", "col"), None),
        P(),
        P(("row", "col"), None, None),
        P(("row", "col"), None, None),
        P(("row", "col"), None),
        P(("row", "col")),
    )
    out_specs = (P(("row", "col"), None), P(("row", "col"), None))
    return jax.shard_map(
        per_device, mesh=mesh, in_specs=in_specs, out_specs=out_specs, check_vma=False
    )
```

profile of v0, /device:TPU:0, one launch (start us, length us, event | category | flops | bytes accessed | tf_op | source)
XLA Modules:
  0.0 254.4 jit_solution(1974750369062565086)
XLA Ops:
  0.6 0.7 and_select_fusion.1
  1.4 0.1 reduce_window_sum.28
  1.5 0.2 select_reduce_fusion
  1.7 0.8 scatter_custom_fusion.1
  2.5 0.7 all_to_all.17
  3.3 7.3 %all-to-all-start.2 = ((s32[32,1,3]{2,1,0:T(1,128)}), s32[32,1,3]{2,1,0:T(1,128)S(1)}, u32[]{:S(2)}, u32[]{:S(2)}) async-start(s32[32,1,3]{2,1,0:T(1,128)} %bitcast.10), calls=%async_computation.2 | async-start | bytes 32768 | tf_op jit(solution)/shard_map/all_to_all | solution.py:55
  10.6 0.8 copy.42
  11.3 0.7 broadcast_multiply_fusion
  12.2 0.6 reduce-window.6
  12.8 0.2 slice_reduce_fusion
  13.2 0.1 mul.55
  13.4 1.2 scatter_custom_fusion
  14.6 0.9 concatenate.6
  15.5 3.1 %gather_fusion = bf16[384,2048]{1,0:T(8,128)(2,1)} fusion(bf16[33,2048]{1,0:T(8,128)(2,1)S(1)} %concatenate.6, s32[1024]{0:T(1024)S(1)} %pad_clamp_fusion.2), kind=kCustom, calls=%fused_computation | custom fusion | bytes 3147264 | tf_op jit(solution)/shard_map/gather | solution.py:85
  18.6 1.8 broadcast_in_dim.18
  20.4 2.9 %reshape.127 = bf16[32,4,6,2048]{3,2,1,0:T(8,128)(2,1)} reshape(bf16[2,384,2048]{2,1,0:T(8,128)(2,1)S(1)} %broadcast_in_dim.18) | data formatting | bytes 6291456 | tf_op jit(solution)/shard_map/reshape | solution.py:87
  23.3 6.8 %copy.45 = bf16[32,4,6,2048]{3,1,2,0:T(4,128)(2,1)} copy(bf16[32,4,6,2048]{3,2,1,0:T(8,128)(2,1)} %reshape.127) | data formatting | bytes 6291456 | tf_op jit(solution)/shard_map/reshape | solution.py:87
  30.2 5.9 %all-to-all-start = ((bf16[32,4,6,2048]{3,1,2,0:T(4,128)(2,1)}), bf16[32,4,6,2048]{3,1,2,0:T(4,128)(2,1)}, u32[]{:S(2)}, u32[]{:S(2)}) async-start(bf16[32,4,6,2048]{3,1,2,0:T(4,128)(2,1)} %copy.45), calls=%async_computation | async-start | bytes 6291456 | tf_op jit(solution)/shard_map/all_to_all | solution.py:90
  36.2 0.8 scatter_custom_fusion.2
  37.0 0.1 concatenate.7
  37.1 1.7 gather_fusion.2
  38.8 2.4 reshape.130
  41.2 66.4 %all-to-all-done = bf16[32,4,6,2048]{3,1,2,0:T(4,128)(2,1)} async-done(((bf16[32,4,6,2048]{3,1,2,0:T(4,128)(2,1)}), bf16[32,4,6,2048]{3,1,2,0:T(4,128)(2,1)}, u32[]{:S(2)}, u32[]{:S(2)}) %all-to-all-start) | async-done | bytes 3145760 | tf_op jit(solution)/shard_map/all_to_all | solution.py:90
  107.6 4.1 %all-to-all-start.3 = ((bf16[32,3,9216]{2,1,0:T(4,128)(2,1)}), bf16[32,3,9216]{2,1,0:T(4,128)(2,1)S(1)}, u32[]{:S(2)}, u32[]{:S(2)}) async-start(bf16[32,3,9216]{2,1,0:T(4,128)(2,1)} %reshape.130), calls=%async_computation.3 | async-start | bytes 4718592 | tf_op jit(solution)/shard_map/all_to_all | solution.py:54
  111.7 17.4 %fusion.4 = f32[32,4,6,1408]{3,0,2,1:T(8,128)S(1)} fusion(bf16[4,2048,1408]{2,1,0:T(8,128)(2,1)} %param.10, bf16[32,4,6,2048]{3,1,2,0:T(4,128)(2,1)} %all-to-all-done), kind=kOutput, calls=%fused_computation.12 | convolution fusion | flops 4429185024 | bytes 30539776 | tf_op jit(solution)/shard_map/ajcd,jdf->ajcf/dot_general | solution.py:21
  129.1 7.1 %fusion.11 = bf16[32,4,6,2048]{3,0,2,1:T(8,128)(2,1)S(1)} fusion(bf16[4,704,2048]{2,1,0:T(8,128)(2,1)} %param.11, f32[32,4,6,1408]{3,0,2,1:T(8,128)S(1)} %fusion.4), kind=kOutput, calls=%fused_computation.16 | convolution fusion | flops 2219409408 | bytes 19398656 | tf_op jit(solution)/shard_map/ajcf,jfd->ajcd/dot_general | solution.py:26
  136.2 4.1 %copy.47 = bf16[32,4,6,2048]{3,1,2,0:T(4,128)(2,1)} copy(bf16[32,4,6,2048]{3,0,2,1:T(8,128)(2,1)S(1)} %fusion.11) | data formatting | bytes 6291456 | tf_op jit(solution)/shard_map/convert_element_type | solution.py:28
  140.3 25.8 %all-to-all-done.3 = bf16[32,3,9216]{2,1,0:T(4,128)(2,1)S(1)} async-done(((bf16[32,3,9216]{2,1,0:T(4,128)(2,1)}), bf16[32,3,9216]{2,1,0:T(4,128)(2,1)S(1)}, u32[]{:S(2)}, u32[]{:S(2)}) %all-to-all-start.3) | async-done | bytes 1769504 | tf_op jit(solution)/shard_map/all_to_all | solution.py:54
  166.1 1.4 copy-done.1
  167.6 4.2 %all-to-all-start.1 = ((bf16[32,4,6,2048]{3,1,2,0:T(4,128)(2,1)}), bf16[32,4,6,2048]{3,1,2,0:T(4,128)(2,1)S(1)}, u32[]{:S(2)}, u32[]{:S(2)}) async-start(bf16[32,4,6,2048]{3,1,2,0:T(4,128)(2,1)} %copy.47), calls=%async_computation.1 | async-start | bytes 6291456 | tf_op jit(solution)/shard_map/all_to_all | solution.py:88
  171.8 0.1 reshape.158
  171.9 1.1 fusion.19
  173.0 1.6 gather_fusion.3
  174.7 0.1 fusion.25
  174.9 0.5 broadcast.171
  175.4 0.7 reduce.5
  176.1 0.1 reshape.129
  176.2 4.5 %reshape.192 = bf16[96,9216]{1,0:T(8,128)(2,1)} reshape(bf16[32,3,9216]{2,1,0:T(4,128)(2,1)} %copy-done.1) | data formatting | bytes 3538944 | tf_op jit(solution)/shard_map/reshape | solution.py:64
  180.7 5.1 %scatter_custom_fusion.3 = bf16[73,9216]{1,0:T(8,128)(2,1)} fusion(s32[96]{0:T(128)S(1)} %fusion.28, bf16[96,9216]{1,0:T(8,128)(2,1)} %reshape.192, bf16[]{:T(256)} %constant.34.clone.1), kind=kCustom, calls=%fused_computation.25 | custom fusion | bytes 1346048 | tf_op jit(solution)/shard_map/scatter | solution.py:64
  185.8 2.5 slice.48
  188.2 54.8 %all-to-all-done.1 = bf16[32,4,6,2048]{3,1,2,0:T(4,128)(2,1)S(1)} async-done(((bf16[32,4,6,2048]{3,1,2,0:T(4,128)(2,1)}), bf16[32,4,6,2048]{3,1,2,0:T(4,128)(2,1)S(1)}, u32[]{:S(2)}, u32[]{:S(2)}) %all-to-all-start.1) | async-done | bytes 3145760 | tf_op jit(solution)/shard_map/all_to_all | solution.py:88
  243.1 2.0 fusion.34
  245.1 1.7 add_convert_fusion
  246.8 2.2 copy.50
  249.0 2.6 %convert_element_type.46 = bf16[384,2048]{1,0:T(8,128)(2,1)S(1)} reshape(bf16[16,4,6,2048]{3,2,1,0:T(8,128)(2,1)} %copy.50) | data formatting | bytes 3145728 | tf_op jit(solution)/shard_map/convert_element_type | solution.py:100
  251.6 1.1 gather_fusion.1
  252.8 0.2 reshape.133
  253.0 1.4 multiply_reduce_fusion
  (28 shorter events, 0.7 us)
Async XLA Ops:
  0.6 171.2 %copy-start = (bf16[2048,64]{0,1:T(8,128)(2,1)S(1)}, bf16[2048,64]{0,1:T(8,128)(2,1)}, u32[]{:S(2)}) copy-start(bf16[2048,64]{0,1:T(8,128)(2,1)} %param.9) | copy-start | bytes 786436
  3.3 26.9 %all-to-all-start.2 = ((s32[32,1,3]{2,1,0:T(1,128)}), s32[32,1,3]{2,1,0:T(1,128)S(1)}, u32[]{:S(2)}, u32[]{:S(2)}) async-start(s32[32,1,3]{2,1,0:T(1,128)} %bitcast.10), calls=%async_computation.2 | async-start | bytes 32768 | tf_op jit(solution)/shard_map/all_to_all | solution.py:55
  30.2 6.8 %copy-start.2 = (bf16[72,9216]{1,0:T(8,128)(2,1)S(1)}, bf16[72,9216]{1,0:T(8,128)(2,1)}, u32[]{:S(2)}) copy-start(bf16[72,9216]{1,0:T(8,128)(2,1)} %param.12) | copy-start | bytes 3981316
  30.2 77.4 %all-to-all-start = ((bf16[32,4,6,2048]{3,1,2,0:T(4,128)(2,1)}), bf16[32,4,6,2048]{3,1,2,0:T(4,128)(2,1)}, u32[]{:S(2)}, u32[]{:S(2)}) async-start(bf16[32,4,6,2048]{3,1,2,0:T(4,128)(2,1)} %copy.45), calls=%async_computation | async-start | bytes 6291456 | tf_op jit(solution)/shard_map/all_to_all | solution.py:90
  107.6 58.5 %all-to-all-start.3 = ((bf16[32,3,9216]{2,1,0:T(4,128)(2,1)}), bf16[32,3,9216]{2,1,0:T(4,128)(2,1)S(1)}, u32[]{:S(2)}, u32[]{:S(2)}) async-start(bf16[32,3,9216]{2,1,0:T(4,128)(2,1)} %reshape.130), calls=%async_computation.3 | async-start | bytes 4718592 | tf_op jit(solution)/shard_map/all_to_all | solution.py:54
  166.1 1.4 copy-start.1
  167.6 75.5 %all-to-all-start.1 = ((bf16[32,4,6,2048]{3,1,2,0:T(4,128)(2,1)}), bf16[32,4,6,2048]{3,1,2,0:T(4,128)(2,1)S(1)}, u32[]{:S(2)}, u32[]{:S(2)}) async-start(bf16[32,4,6,2048]{3,1,2,0:T(4,128)(2,1)} %copy.47), calls=%async_computation.1 | async-start | bytes 6291456 | tf_op jit(solution)/shard_map/all_to_all | solution.py:88
where the time goes:
time: 255 us; the launch traced here: 254 us
  waiting for transfers between devices  147 us (58%)
  local copies, waits for them, and re-layouts  52.7 us (21%)
  matrix products  25.6 us (10%)
  starting transfers between devices  21.5 us (8%)
  other arithmetic  6.57 us (3%)
    all_to_all x1, waiting for transfers between devices, per_device(): lax.all_to_all(outgoing, ('row', 'col'), split_axis=0, concat_axis=0, til...  66.4 us
    all_to_all x1, waiting for transfers between devices, per_device(): lax.all_to_all(expert_halves(lax.all_to_all(outgoing, ('row', 'col'), spl...  54.8 us
    all_to_all x1, waiting for transfers between devices, move_pages(): lax.all_to_all(outgoing, ('row', 'col'), split_axis=0, concat_axis=0, til...  25.8 us
    dot_general x1, matrix products, expert_halves(): jnp.einsum('ajcd,jdf->ajcf', buffer, w_in, preferred_element_type=jnp.flo...  17.4 us
    reshape x2, local copies, waits for them, and re-layouts, per_device(): outgoing = outgoing.reshape(devices, halves_here, CAPE, model_width)  9.75 us
    all_to_all x1, starting transfers between devices, move_pages(): lax.all_to_all(landing.reshape(devices, page_cap), ('row', 'col'), split_...  7.3 us
    dot_general x1, matrix products, expert_halves(): jnp.einsum('ajcf,jfd->ajcd', activated, w_out, preferred_element_type=jnp...  7.11 us
    all_to_all x1, starting transfers between devices, per_device(): lax.all_to_all(outgoing, ('row', 'col'), split_axis=0, concat_axis=0, til...  5.95 us
  transfers between devices with their start and end apart: 4, of which 3 were waited for; matrix products, arithmetic and copies ran while one was open for 27% of the time, Pallas kernels for 0%

commit v1 on v0

v1 whole, which is shorter than its diff:
```python
import functools

import jax
import jax.numpy as jnp
from jax import lax
from jax.experimental import pallas as pl
from jax.experimental.pallas import tpu as pltpu
from jax.sharding import PartitionSpec as P

EXPERTS = 64
CAPE = 6
AXES = ("row", "col")
ROUTE_SCALE = 2.446
CHUNK = 512


def experts_kernel(base_ref, x_ref, router_ref, routes_ref, w_in_ref, w_out_ref, out_ref,
                   gates, ranks, weighted):
    step = pl.program_id(0)
    steps = pl.num_programs(0)
    count = x_ref.shape[0]
    rows = weighted.shape[1]
    hidden = w_out_ref.shape[1]

    @pl.when(step == 0)
    def _():
        expert_row = lax.broadcasted_iota(jnp.int32, (EXPERTS, CHUNK), 0)
        earlier = (
            lax.broadcasted_iota(jnp.int32, (CHUNK, CHUNK), 0)
            < lax.broadcasted_iota(jnp.int32, (CHUNK, CHUNK), 1)
        ).astype(jnp.float32).astype(jnp.bfloat16)
        offset = jnp.zeros((EXPERTS, 1), jnp.float32)
        for begin in range(0, count, CHUNK):
            part = slice(begin, begin + CHUNK)
            logits = lax.dot_general(
                router_ref[...], x_ref[part, :], (((1,), (1,)), ((), ())),
                preferred_element_type=jnp.float32,
            )
            scores = 1.0 / (1.0 + jnp.exp(-logits))
            named = jnp.zeros((EXPERTS, CHUNK), jnp.float32)
            for k in range(routes_ref.shape[0]):
                named = jnp.where(routes_ref[k : k + 1, part] == expert_row, 1.0, named)
            picked = scores * named
            gates[:, part] = ROUTE_SCALE * picked / jnp.sum(picked, axis=0, keepdims=True)
            before = offset + jnp.dot(
                named.astype(jnp.bfloat16), earlier, preferred_element_type=jnp.float32
            )
            ranks[:, part] = jnp.where(named > 0.0, before, -1.0)
            offset = offset + jnp.sum(named, axis=1, keepdims=True)

    expert = base_ref[0] + step

    def chosen(which, part):
        slots = lax.broadcasted_iota(jnp.int32, (rows, part.size), 0).astype(jnp.float32)
        return ranks[pl.ds(which, 1), part] == slots

    picked_rows = jnp.zeros((rows, x_ref.shape[1]), jnp.float32)
    row_gate = jnp.zeros((rows, 1), jnp.float32)
    for begin in range(0, count, CHUNK):
        part = pl.ds(begin, CHUNK)
        hit = chosen(expert, part)
        picked_rows += jnp.dot(
            hit.astype(jnp.float32).astype(jnp.bfloat16), x_ref[part, :],
            preferred_element_type=jnp.float32,
        )
        row_gate += jnp.sum(
            jnp.where(hit, gates[pl.ds(expert, 1), part], 0.0), axis=1, keepdims=True
        )
    gate_up = jnp.dot(
        picked_rows.astype(jnp.bfloat16), w_in_ref[0], preferred_element_type=jnp.float32
    )
    gate = gate_up[:, :hidden]
    activated = (gate / (1.0 + jnp.exp(-gate)) * gate_up[:, hidden:]).astype(jnp.bfloat16)
    half = jnp.dot(activated, w_out_ref[0], preferred_element_type=jnp.float32)
    weighted[pl.ds(step, 1)] = (half * row_gate).astype(jnp.bfloat16)[None]

    @pl.when(step == steps - 1)
    def _():
        for begin in range(0, count, CHUNK):
            part = pl.ds(begin, CHUNK)
            hits = jnp.concatenate(
                [
                    chosen(base_ref[0] + j, part).astype(jnp.float32).astype(jnp.bfloat16)
                    for j in range(weighted.shape[0])
                ],
                axis=0,
            )
            out_ref[part, :] = lax.dot_general(
                hits, weighted[...].reshape(-1, weighted.shape[2]),
                (((0,), (0,)), ((), ())), preferred_element_type=jnp.float32,
            ).astype(jnp.bfloat16)


def run_experts(base, x, router_t, routes_t, w_in, w_out, devices):
    count, width = x.shape
    halves_here, hidden, _ = w_out.shape
    rows = CAPE * devices
    whole = functools.partial(pl.BlockSpec, pipeline_mode=pl.Buffered(1))
    return pl.pallas_call(
        experts_kernel,
        grid=(halves_here,),
        in_specs=[
            pl.BlockSpec(memory_space=pltpu.SMEM),
            whole((count, width), lambda j: (0, 0)),
            whole(router_t.shape, lambda j: (0, 0)),
            whole(routes_t.shape, lambda j: (0, 0)),
            pl.BlockSpec((1,) + w_in.shape[1:], lambda j: (j, 0, 0)),
            pl.BlockSpec((1,) + w_out.shape[1:], lambda j: (j, 0, 0)),
        ],
        out_specs=whole((count, width), lambda j: (0, 0)),
        out_shape=jax.ShapeDtypeStruct((count, width), jnp.bfloat16),
        scratch_shapes=[
            pltpu.VMEM((EXPERTS, count), jnp.float32),
            pltpu.VMEM((EXPERTS, count), jnp.float32),
            pltpu.VMEM((halves_here, rows, width), jnp.bfloat16),
        ],
        compiler_params=pltpu.CompilerParams(vmem_limit_bytes=60 << 20),
        cost_estimate=pl.CostEstimate(
            flops=20 * 10**9, bytes_accessed=45 * 10**6, transcendentals=10**6
        ),
    )(base, x, router_t, routes_t, w_in, w_out)


def per_device(tokens, routes, router, w_in, w_out, cache_prefill, page_slot):
    devices = lax.axis_size(AXES)
    me = lax.axis_index(AXES)
    pages_here, page_width = cache_prefill.shape
    page_cap = pages_here // devices + 1
    tok_count, top_count = routes.shape
    halves_here = w_in.shape[0]

    target = page_slot // pages_here
    same = target[:, None] == target[None, :]
    earlier = jnp.arange(pages_here)[None, :] < jnp.arange(pages_here)[:, None]
    placed = target * page_cap + jnp.sum((same & earlier).astype(jnp.int32), axis=1)
    send_pick = (jnp.arange(devices * page_cap)[:, None] == placed[None, :]).astype(jnp.bfloat16)
    outgoing = jnp.dot(send_pick, cache_prefill, preferred_element_type=jnp.float32).astype(
        jnp.bfloat16
    )
    arrived = lax.all_to_all(outgoing, AXES, split_axis=0, concat_axis=0, tiled=True)

    numbers = jnp.concatenate([routes.reshape(-1), page_slot])
    numbers = lax.all_gather(numbers[None], AXES, axis=0, tiled=True)
    x = lax.all_gather(tokens, AXES, axis=0, tiled=True)
    all_routes = numbers[:, : tok_count * top_count].reshape(devices * tok_count, top_count)
    base = jnp.reshape((me * halves_here) % EXPERTS, (1,)).astype(jnp.int32)
    partial = run_experts(base, x, router.T, all_routes.T, w_in, w_out, devices)
    moe_out = lax.psum_scatter(partial, AXES, scatter_dimension=0, tiled=True)

    slots = numbers[:, tok_count * top_count :]
    mine = slots // pages_here == me
    order = jnp.sum((mine[:, None, :] & earlier[None]).astype(jnp.int32), axis=2)
    taken = mine[:, None, :] & (order[:, None, :] == jnp.arange(page_cap)[None, :, None])
    landing = jnp.sum(jnp.where(taken, slots[:, None, :] % pages_here + 1, 0), axis=2) - 1
    land_pick = (jnp.arange(pages_here)[:, None] == landing.reshape(1, -1)).astype(jnp.bfloat16)
    cache_decode = jnp.dot(land_pick, arrived, preferred_element_type=jnp.float32).astype(
        jnp.bfloat16
    )
    return moe_out, cache_decode


def solution(mesh):
    in_specs = (
        P(AXES, None),
        P(AXES, None),
        P(),
        P(AXES, None, None),
        P(AXES, None, None),
        P(AXES, None),
        P(AXES),
    )
    out_specs = (P(AXES, None), P(AXES, None))
    return jax.shard_map(
        per_device, mesh=mesh, in_specs=in_specs, out_specs=out_specs, check_vma=False
    )
```

time: 255 us -> 253 us (level)
  local copies, waits for them, and re-layouts: 52.7 us -> 8.96 us
  blocking collectives: 0 us -> 43.1 us
  Pallas kernels: 0 us -> 24.3 us
  matrix products: 25.6 us -> 2.18 us
  starting transfers between devices: 21.5 us -> 3.6 us
  between operations: 0.96 us -> 14.2 us
  waiting for transfers between devices: 147 us -> 154 us
  other arithmetic: 6.57 us -> 2.01 us
    all_to_all x4 -> x1, waiting for transfers between devices: 147 us -> 61.1 us  [per_device(): lax.all_to_all(outgoing, AXES, split_axis=0, concat_axis=0, tiled=True)]
    reduce_scatter x0 -> x1, waiting for transfers between devices: none -> 70.8 us  [per_device(): moe_out = lax.psum_scatter(partial, AXES, scatter_dimension=0, tiled=True)]
    unnamed x0 -> x1, blocking collectives: none -> 43.1 us
    pallas_call x0 -> x1, Pallas kernels: none -> 24.3 us  [run_experts(): pl.pallas_call(experts_kernel, grid=(halves_here,), in_specs=[pl.BlockSpe...]
    dot_general x3 -> x2, matrix products: 25.6 us -> 2.18 us  [the longest x1 1.56 us: per_device(): jnp.dot(land_pick, arrived, preferred_element_type=jnp.float32)]
    all_gather x0 -> x1, waiting for transfers between devices: none -> 21.3 us  [per_device(): x = lax.all_gather(tokens, AXES, axis=0, tiled=True)]
    all_to_all x4 -> x1, starting transfers between devices: 21.5 us -> 3.52 us  [per_device(): lax.all_to_all(outgoing, AXES, split_axis=0, concat_axis=0, tiled=True)]
    reshape x5 -> x3, local copies, waits for them, and re-layouts: 16.7 us -> 1.45 us  [the longest x2 1.35 us: per_device(): numbers[:, :tok_count * top_count].reshape(devices * tok_count, top_count)]
  transfers between devices with their start and end apart: 4 -> 3, of which waited for: 3 -> 3; matrix products, arithmetic and copies ran while one was open for 27% -> 3% of each run, Pallas kernels for 0% -> 0%
where the time goes in v1:
time: 253 us; the launch traced here: 252 us
  waiting for transfers between devices  154 us (61%)
  blocking collectives  43.1 us (17%)
  Pallas kernels  24.3 us (10%)
  between operations  14.2 us (6%)
  local copies, waits for them, and re-layouts  8.96 us (4%)
  starting transfers between devices  3.6 us (1%)
    reduce_scatter x1, waiting for transfers between devices, per_device(): moe_out = lax.psum_scatter(partial, AXES, scatter_dimension=0, tiled=True)  70.8 us
    all_to_all x1, waiting for transfers between devices, per_device(): lax.all_to_all(outgoing, AXES, split_axis=0, concat_axis=0, tiled=True)  61.1 us
    unnamed x1, blocking collectives  43.1 us
    pallas_call x1, Pallas kernels, run_experts(): pl.pallas_call(experts_kernel, grid=(halves_here,), in_specs=[pl.BlockSpe...  24.3 us
    all_gather x1, waiting for transfers between devices, per_device(): x = lax.all_gather(tokens, AXES, axis=0, tiled=True)  21.3 us
    all_to_all x2, local copies, waits for them, and re-layouts, per_device(): lax.all_to_all(outgoing, AXES, split_axis=0, concat_axis=0, tiled=True)  5.8 us
  transfers between devices with their start and end apart: 3, of which 3 were waited for; matrix products, arithmetic and copies ran while one was open for 3% of the time, Pallas kernels for 0%

profile of v1, /device:TPU:0, one launch (start us, length us, event | category | flops | bytes accessed | tf_op | source)
XLA Modules:
  0.0 252.3 jit_solution(4567325780364912395)
XLA Ops:
  7.2 0.0 copy-start
  7.2 0.0 all-gather.3.cloned.1.call-start
  7.2 0.7 all-gather.3.cloned.1.call-update
  7.9 0.0 reduce-scatter.2.cloned.1.call-start
  8.0 0.8 copy.11
  8.7 0.1 reshape.49
  8.9 0.8 add_dynamic-update-slice_fusion
  9.7 43.1 %all-reduce = s32[8448]{0:T(1024)S(1)} all-reduce(s32[8448]{0:T(1024)S(1)} %add_dynamic-update-slice_fusion), channel_id=2, replica_groups=mesh['row'=4,'col'=8] {'row','col'}, use_global_device_ids=true, to_apply=%add | all-reduce | flops 8448 | bytes 67584
  52.8 0.1 reshape.51
  53.0 0.5 reshape.50
  53.5 0.8 copy.12
  54.3 21.3 %all-gather.3.cloned.1.call-done.x_ref = bf16[1024,2048]{1,0:T(8,128)(2,1)} async-done(((bf16[32,2048]{1,0:T(8,128)(2,1)}), bf16[1024,2048]{1,0:T(8,128)(2,1)}) %all-gather.3.cloned.1.call-update) | async-done | bytes 4194320 | tf_op jit(solution)/shard_map/all_gather | solution.py:144
  75.6 24.3 %shard_map.86 = bf16[1024,2048]{1,0:T(8,128)(2,1)} custom-call(s32[1]{0:T(128)} %bitcast.base_ref, bf16[1024,2048]{1,0:T(8,128)(2,1)} %all-gather.3.cloned.1.call-done.x_ref, bf16[64,2048]{1,0:T(8,128)(2,1)} %bitcast.6, s32[6,1024]{1,0:T(8,128)} %bitcast.5, bf16[4,2048,1408]{2,1,0:T(8,128)(2,1)} %w_in_ref.1, bf16[4,704,2048]{2,1,0:T(8,128)(2,1)} %w_out_ref.1), custom_call_target="tpu_custom_call" | custom-call | flops 20000000000 | bytes 45000000 | tf_op jit(solution)/shard_map/pallas_call | solution.py:99
  99.9 0.0 copy-start.1
  99.9 0.0 reduce-scatter.2.cloned.1.call-update
  99.9 0.6 copy-done.1
  100.6 0.2 convert_reduce_fusion.1
  100.8 0.0 copy-done
  100.8 0.6 convolution_convert_fusion
  101.4 2.5 all_to_all.8
  103.9 3.5 %all-to-all-start = ((bf16[32,3,9216]{2,1,0:T(4,128)(2,1)}), bf16[32,3,9216]{2,1,0:T(4,128)(2,1)}, u32[]{:S(2)}, u32[]{:S(2)}) async-start(bf16[32,3,9216]{2,1,0:T(4,128)(2,1)} %all_to_all.8), calls=%async_computation.1 | async-start | bytes 4718592 | tf_op jit(solution)/shard_map/all_to_all | solution.py:140
  107.4 0.1 fusion.3
  107.5 0.6 convert_reduce_fusion
  108.2 0.1 fusion.4
  108.3 0.1 select_reduce_fusion
  108.4 0.1 copy.13
  108.5 0.1 sub.20
  108.6 61.1 %all-to-all-done = bf16[32,3,9216]{2,1,0:T(4,128)(2,1)} async-done(((bf16[32,3,9216]{2,1,0:T(4,128)(2,1)}), bf16[32,3,9216]{2,1,0:T(4,128)(2,1)}, u32[]{:S(2)}, u32[]{:S(2)}) %all-to-all-start) | async-done | bytes 1769504 | tf_op jit(solution)/shard_map/all_to_all | solution.py:140
  169.7 3.3 %all_to_all.10 = bf16[96,9216]{1,0:T(8,128)(2,1)S(1)} reshape(bf16[32,3,9216]{2,1,0:T(4,128)(2,1)} %all-to-all-done) | data formatting | bytes 3538944 | tf_op jit(solution)/shard_map/all_to_all | solution.py:140
  173.1 1.6 convolution_convert_fusion.1
  174.6 70.8 %reduce-scatter.2.cloned.1.call-done = bf16[32,2048]{1,0:T(8,128)(2,1)} async-done(((bf16[1024,2048]{1,0:T(8,128)(2,1)}), bf16[32,2048]{1,0:T(8,128)(2,1)}) %reduce-scatter.2.cloned.1.call-update) | async-done | bytes 131088 | tf_op jit(solution)/shard_map/reduce_scatter | solution.py:148
  (6 shorter events, 0.1 us)
Async XLA Ops:
  7.2 93.6 %copy-start = (bf16[72,9216]{1,0:T(8,128)(2,1)S(1)}, bf16[72,9216]{1,0:T(8,128)(2,1)}, u32[]{:S(2)}) copy-start(bf16[72,9216]{1,0:T(8,128)(2,1)} %param.12) | copy-start | bytes 3981316
  7.2 68.5 %all-gather.3.cloned.1.call-start = ((), (), s32[]{:S(2)}) async-start(), calls=%async_computation.2 | async-start | bytes 4325376 | tf_op jit(solution)/shard_map/all_gather | solution.py:144
  7.9 237.6 %reduce-scatter.2.cloned.1.call-start = ((), (), s32[]{:S(2)}) async-start(), calls=%async_computation.3 | async-start | bytes 4325376 | tf_op jit(solution)/shard_map/reduce_scatter | solution.py:148
  99.9 0.7 copy-start.1
  103.9 65.8 %all-to-all-start = ((bf16[32,3,9216]{2,1,0:T(4,128)(2,1)}), bf16[32,3,9216]{2,1,0:T(4,128)(2,1)}, u32[]{:S(2)}, u32[]{:S(2)}) async-start(bf16[32,3,9216]{2,1,0:T(4,128)(2,1)} %all_to_all.8), calls=%async_computation.1 | async-start | bytes 4718592 | tf_op jit(solution)/shard_map/all_to_all | solution.py:140
Sparse Core Ops, SparseCore 0:
  10.9 64.7 all-gather.2
  100.1 145.3 reduce-scatter.1

commit v2 on v1

--- a/solution.py
+++ b/solution.py
@@ -12,6 +12,9 @@
 AXES = ("row", "col")
 ROUTE_SCALE = 2.446
 CHUNK = 512
+TOP = 6
+MESH = pl.DeviceIdType.MESH
+FUSED_TOKENS = 1024
 
 
 def experts_kernel(base_ref, x_ref, router_ref, routes_ref, w_in_ref, w_out_ref, out_ref,
@@ -121,6 +124,269 @@
     )(base, x, router_t, routes_t, w_in, w_out)
 
 
+def bits_of(number, count):
+    return [(number // 2 ** (count - 1 - b)) % 2 for b in range(count)]
+
+
+def fused_kernel(n_row, n_col, tokens_ref, router_ref, numbers_ref, pages_ref, w_in_hbm, w_out_hbm,
+                 out_ref, arrived_ref, all_numbers_ref,
+                 x, part, gates, ranks, weighted, w_in_buf, w_out_buf, *rest):
+    devices = n_row * n_col
+    dims = devices.bit_length() - 1
+    row_bits = n_row.bit_length() - 1
+    sends, receives = rest[:dims], rest[dims : 2 * dims]
+    (w_sem, own_sem, page_send, page_recv, gather_send, gather_recv,
+     sum_send, sum_recv) = rest[2 * dims :]
+    row, col = lax.axis_index("row"), lax.axis_index("col")
+    me = row * n_col + col
+    mine = bits_of(me, dims)
+    tok_count, width = tokens_ref.shape
+    halves_here, hidden, _ = w_out_hbm.shape
+    rows = weighted.shape[1]
+    split = width // 2
+    columns = [pl.ds(0, split), pl.ds(split, split)]
+    inner = list(range(row_bits, dims - 1))
+    orders = [
+        list(range(row_bits)) + inner + [dims - 1],
+        list(range(row_bits)) + inner[::-1] + [dims - 1],
+    ]
+
+    def place(number):
+        return (number // n_col, number % n_col)
+
+    def partner(b):
+        return place(me + (1 - 2 * mine[b]) * 2 ** (dims - 1 - b))
+
+    def weights(j, slot):
+        return (
+            pltpu.make_async_copy(w_in_hbm.at[j], w_in_buf.at[slot], w_sem.at[slot, 0]),
+            pltpu.make_async_copy(w_out_hbm.at[j], w_out_buf.at[slot], w_sem.at[slot, 1]),
+        )
+
+    slots = w_in_buf.shape[0]
+    for j in range(min(slots, halves_here)):
+        for copy in weights(j, j):
+            copy.start()
+    own = pltpu.make_async_copy(pages_ref.at[me], arrived_ref.at[me], own_sem)
+    own.start()
+
+    barrier = pltpu.get_barrier_semaphore()
+
+    @pl.loop(1, devices)
+    def _(o):
+        pl.semaphore_signal(barrier, inc=1, device_id=place((me + o) % devices), device_id_type=MESH)
+
+    x[tuple(mine)] = tokens_ref[...]
+    all_numbers_ref[tuple(mine)] = numbers_ref[...]
+    pl.semaphore_wait(barrier, devices - 1)
+
+    def page(o):
+        to = (me + o) % devices
+        return pltpu.make_async_remote_copy(
+            src_ref=pages_ref.at[to], dst_ref=arrived_ref.at[me],
+            send_sem=page_send.at[o], recv_sem=page_recv.at[o],
+            device_id=place(to), device_id_type=MESH,
+        )
+
+    for s in range(dims):
+        copies = []
+        for h in range(3):
+            order = orders[h % 2]
+            done, b = order[:s], order[s]
+            index = tuple(slice(None) if d in done else mine[d] for d in range(dims))
+            if h < 2:
+                ref = x.at[index + (slice(None), columns[h])]
+            else:
+                ref = all_numbers_ref.at[index]
+            copies.append(
+                pltpu.make_async_remote_copy(
+                    src_ref=ref, dst_ref=ref,
+                    send_sem=gather_send.at[s, h], recv_sem=gather_recv.at[s, h],
+                    device_id=partner(b), device_id_type=MESH,
+                )
+            )
+        for copy in copies:
+            copy.start()
+        for copy in copies:
+            copy.wait()
+        if s == row_bits - 1:
+
+            @pl.loop(1, devices)
+            def _(o):
+                page(o).start()
+
+    chunk = devices // 2 * tok_count
+    group = 128 // tok_count
+
+    def tokens_of(q):
+        return x[q].reshape(chunk, width)
+
+    expert_row = lax.broadcasted_iota(jnp.int32, (EXPERTS, chunk), 0)
+    earlier = (
+        lax.broadcasted_iota(jnp.int32, (chunk, chunk), 0)
+        < lax.broadcasted_iota(jnp.int32, (chunk, chunk), 1)
+    ).astype(jnp.float32).astype(jnp.bfloat16)
+    offset = jnp.zeros((EXPERTS, 1), jnp.float32)
+    for q in range(2):
+        part_q = slice(q * chunk, (q + 1) * chunk)
+        numbers = all_numbers_ref[q].reshape(-1, group, 8, 128)
+        numbers = [
+            functools.reduce(lambda a, b: a + b, [numbers[i, g] for g in range(group)])
+            for i in range(numbers.shape[0])
+        ]
+        routes = jnp.concatenate(numbers, axis=1)
+        logits = lax.dot_general(
+            router_ref[...], tokens_of(q), (((1,), (1,)), ((), ())),
+            preferred_element_type=jnp.float32,
+        )
+        scores = 1.0 / (1.0 + jnp.exp(-logits))
+        named = jnp.zeros((EXPERTS, chunk), jnp.float32)
+        for k in range(TOP):
+            named = jnp.where(routes[k : k + 1, :] == expert_row, 1.0, named)
+        picked = scores * named
+        gates[:, part_q] = ROUTE_SCALE * picked / jnp.sum(picked, axis=0, keepdims=True)
+        before = offset + jnp.dot(
+            named.astype(jnp.bfloat16), earlier, preferred_element_type=jnp.float32
+        )
+        ranks[:, part_q] = jnp.where(named > 0.0, before, -1.0)
+        offset = offset + jnp.sum(named, axis=1, keepdims=True)
+
+    base = (me * halves_here) % EXPERTS
+
+    def chosen(which, q):
+        numbering = lax.broadcasted_iota(jnp.int32, (rows, chunk), 0).astype(jnp.float32)
+        return ranks[pl.ds(which, 1), q * chunk : (q + 1) * chunk] == numbering
+
+    @pl.loop(0, halves_here)
+    def _(j):
+        slot = j % slots
+        expert = base + j
+        picked_rows = jnp.zeros((rows, width), jnp.float32)
+        row_gate = jnp.zeros((rows, 1), jnp.float32)
+        for q in range(2):
+            hit = chosen(expert, q)
+            picked_rows += jnp.dot(
+                hit.astype(jnp.float32).astype(jnp.bfloat16), tokens_of(q),
+                preferred_element_type=jnp.float32,
+            )
+            row_gate += jnp.sum(
+                jnp.where(hit, gates[pl.ds(expert, 1), q * chunk : (q + 1) * chunk], 0.0),
+                axis=1, keepdims=True,
+            )
+        w_first, w_second = weights(j, slot)
+        w_first.wait()
+        gate_up = jnp.dot(
+            picked_rows.astype(jnp.bfloat16), w_in_buf[slot], preferred_element_type=jnp.float32
+        )
+        gate = gate_up[:, :hidden]
+        activated = (gate / (1.0 + jnp.exp(-gate)) * gate_up[:, hidden:]).astype(jnp.bfloat16)
+        w_second.wait()
+        half = jnp.dot(activated, w_out_buf[slot], preferred_element_type=jnp.float32)
+        weighted[pl.ds(j, 1)] = (half * row_gate).astype(jnp.bfloat16)[None]
+
+        @pl.when(j + slots < halves_here)
+        def _():
+            for copy in weights(j + slots, slot):
+                copy.start()
+
+    for q in range(2):
+        hits = jnp.concatenate(
+            [
+                chosen(base + j, q).astype(jnp.float32).astype(jnp.bfloat16)
+                for j in range(halves_here)
+            ],
+            axis=0,
+        )
+        part[pl.ds(q * (devices // 2), devices // 2)] = lax.dot_general(
+            hits, weighted[...].reshape(halves_here * rows, width),
+            (((0,), (0,)), ((), ())), preferred_element_type=jnp.float32,
+        ).reshape(devices // 2, tok_count, width)
+
+    def blocks(order, s, flip):
+        fixed = {b: mine[b] for b in order[:s]}
+        fixed[order[s]] = 1 - mine[order[s]] if flip else mine[order[s]]
+        free = sorted(order[s + 1 :])
+        for i in range(2 ** len(free)):
+            bits = dict(fixed)
+            for place_of, d in enumerate(free):
+                bits[d] = (i >> (len(free) - 1 - place_of)) & 1
+            yield i, sum(bits[d] * 2 ** (dims - 1 - d) for d in range(dims))
+
+    for s in range(dims):
+        copies = []
+        for h in range(2):
+            order = orders[h][::-1]
+            for i, block in blocks(order, s, True):
+                sends[s][i, :, columns[h]] = part[block, :, columns[h]].astype(jnp.bfloat16)
+            copy = pltpu.make_async_remote_copy(
+                src_ref=sends[s].at[:, :, columns[h]], dst_ref=receives[s].at[:, :, columns[h]],
+                send_sem=sum_send.at[s, h], recv_sem=sum_recv.at[s, h],
+                device_id=partner(order[s]), device_id_type=MESH,
+            )
+            copy.start()
+            copies.append(copy)
+        for h in range(2):
+            copies[h].wait()
+            for i, block in blocks(orders[h][::-1], s, False):
+                part[block, :, columns[h]] += receives[s][i, :, columns[h]].astype(jnp.float32)
+    out_ref[...] = part[me].astype(jnp.bfloat16)
+
+    own.wait()
+
+    @pl.loop(1, devices)
+    def _(o):
+        page(o).wait()
+
+
+def run_fused(n_row, n_col, tokens, router_t, numbers, pages, w_in, w_out):
+    devices = n_row * n_col
+    dims = devices.bit_length() - 1
+    tok_count, width = tokens.shape
+    halves_here, hidden, _ = w_out.shape
+    count = devices * tok_count
+    rows = CAPE * devices
+    cube = (2,) * dims
+    slots = min(2, halves_here)
+    vmem = pl.BlockSpec(memory_space=pltpu.VMEM)
+    anywhere = pl.BlockSpec(memory_space=pl.ANY)
+    parts = [pltpu.VMEM((2 ** (dims - 1 - s), tok_count, width), jnp.bfloat16) for s in range(dims)]
+    return pl.pallas_call(
+        functools.partial(fused_kernel, n_row, n_col),
+        in_specs=[vmem, vmem, vmem, anywhere, anywhere, anywhere],
+        out_specs=[vmem, anywhere, vmem],
+        out_shape=[
+            jax.ShapeDtypeStruct((tok_count, width), jnp.bfloat16),
+            jax.ShapeDtypeStruct(pages.shape, jnp.bfloat16),
+            jax.ShapeDtypeStruct(cube + numbers.shape, jnp.int32),
+        ],
+        scratch_shapes=[
+            pltpu.VMEM(cube + (tok_count, width), jnp.bfloat16),
+            pltpu.VMEM((devices, tok_count, width), jnp.float32),
+            pltpu.VMEM((EXPERTS, count), jnp.float32),
+            pltpu.VMEM((EXPERTS, count), jnp.float32),
+            pltpu.VMEM((halves_here, rows, width), jnp.bfloat16),
+            pltpu.VMEM((slots,) + w_in.shape[1:], jnp.bfloat16),
+            pltpu.VMEM((slots,) + w_out.shape[1:], jnp.bfloat16),
+            *parts,
+            *parts,
+            pltpu.SemaphoreType.DMA((slots, 2)),
+            pltpu.SemaphoreType.DMA(()),
+            pltpu.SemaphoreType.DMA((devices,)),
+            pltpu.SemaphoreType.DMA((devices,)),
+            pltpu.SemaphoreType.DMA((dims, 3)),
+            pltpu.SemaphoreType.DMA((dims, 3)),
+            pltpu.SemaphoreType.DMA((dims, 2)),
+            pltpu.SemaphoreType.DMA((dims, 2)),
+        ],
+        compiler_params=pltpu.CompilerParams(
+            collective_id=0, has_side_effects=True, vmem_limit_bytes=60 << 20
+        ),
+        cost_estimate=pl.CostEstimate(
+            flops=20 * 10**9, bytes_accessed=45 * 10**6, transcendentals=10**6
+        ),
+    )(tokens, router_t, numbers, pages, w_in, w_out)
+
+
 def per_device(tokens, routes, router, w_in, w_out, cache_prefill, page_slot):
     devices = lax.axis_size(AXES)
     me = lax.axis_index(AXES)
@@ -137,17 +403,39 @@
     outgoing = jnp.dot(send_pick, cache_prefill, preferred_element_type=jnp.float32).astype(
         jnp.bfloat16
     )
-    arrived = lax.all_to_all(outgoing, AXES, split_axis=0, concat_axis=0, tiled=True)
-
-    numbers = jnp.concatenate([routes.reshape(-1), page_slot])
-    numbers = lax.all_gather(numbers[None], AXES, axis=0, tiled=True)
-    x = lax.all_gather(tokens, AXES, axis=0, tiled=True)
-    all_routes = numbers[:, : tok_count * top_count].reshape(devices * tok_count, top_count)
-    base = jnp.reshape((me * halves_here) % EXPERTS, (1,)).astype(jnp.int32)
-    partial = run_experts(base, x, router.T, all_routes.T, w_in, w_out, devices)
-    moe_out = lax.psum_scatter(partial, AXES, scatter_dimension=0, tiled=True)
-
-    slots = numbers[:, tok_count * top_count :]
+    if devices * tok_count <= FUSED_TOKENS and tok_count * 4 <= 128:
+        pad = -(page_cap * page_width) % (16 * 128)
+        pages = outgoing.reshape(devices, page_cap * page_width)
+        pages = jnp.pad(pages, ((0, 0), (0, pad))).reshape(devices, -1, 128)
+        lane = jnp.arange(128) // tok_count
+        spread = jnp.tile(routes.T, (1, 128 // tok_count))
+        spread = jnp.where(lane[None, :] == me % (128 // tok_count), spread, 0)
+        block = jnp.concatenate(
+            [
+                spread,
+                jnp.pad(page_slot, (0, 128 - pages_here))[None],
+                jnp.zeros((7 - top_count, 128), jnp.int32),
+            ],
+            axis=0,
+        )
+        moe_out, arrived, numbers = run_fused(
+            lax.axis_size("row"), lax.axis_size("col"), tokens, router.T, block, pages, w_in, w_out
+        )
+        arrived = arrived.reshape(devices, -1)[:, : page_cap * page_width]
+        arrived = arrived.reshape(devices * page_cap, page_width)
+        slots = numbers.reshape(devices, 8, 128)[:, top_count, :pages_here]
+    else:
+        arrived = lax.all_to_all(outgoing, AXES, split_axis=0, concat_axis=0, tiled=True)
+
+        numbers = jnp.concatenate([routes.reshape(-1), page_slot])
+        numbers = lax.all_gather(numbers[None], AXES, axis=0, tiled=True)
+        x = lax.all_gather(tokens, AXES, axis=0, tiled=True)
+        all_routes = numbers[:, : tok_count * top_count].reshape(devices * tok_count, top_count)
+        base = jnp.reshape((me * halves_here) % EXPERTS, (1,)).astype(jnp.int32)
+        partial = run_experts(base, x, router.T, all_routes.T, w_in, w_out, devices)
+        moe_out = lax.psum_scatter(partial, AXES, scatter_dimension=0, tiled=True)
+        slots = numbers[:, tok_count * top_count :]
+
     mine = slots // pages_here == me
     order = jnp.sum((mine[:, None, :] & earlier[None]).astype(jnp.int32), axis=2)
     taken = mine[:, None, :] & (order[:, None, :] == jnp.arange(page_cap)[None, :, None])

time: 253 us -> 146 us (0.58)
  waiting for transfers between devices: 154 us -> 0 us
  Pallas kernels: 24.3 us -> 125 us
  blocking collectives: 43.1 us -> 0 us
  between operations: 14.2 us -> 0.75 us
  local copies, waits for them, and re-layouts: 8.96 us -> 14.3 us
  starting transfers between devices: 3.6 us -> 0 us
    pallas_call x1, Pallas kernels: 24.3 us -> 125 us  [run_fused(): pl.pallas_call(functools.partial(fused_kernel, n_row, n_col), in_specs=[v...]
    reduce_scatter x1 -> x0, waiting for transfers between devices: 70.8 us -> none  [per_device(): moe_out = lax.psum_scatter(partial, AXES, scatter_dimension=0, tiled=True)]
    all_to_all x1 -> x0, waiting for transfers between devices: 61.1 us -> none  [per_device(): lax.all_to_all(outgoing, AXES, split_axis=0, concat_axis=0, tiled=True)]
    unnamed x1 -> x0, blocking collectives: 43.1 us -> none
    all_gather x1 -> x0, waiting for transfers between devices: 21.3 us -> none  [per_device(): x = lax.all_gather(tokens, AXES, axis=0, tiled=True)]
    all_to_all x2 -> x0, local copies, waits for them, and re-layouts: 5.8 us -> none  [per_device(): lax.all_to_all(outgoing, AXES, split_axis=0, concat_axis=0, tiled=True)]
    unnamed x6 -> x8, local copies, waits for them, and re-layouts: 1.41 us -> 5.97 us
    all_to_all x1 -> x0, starting transfers between devices: 3.52 us -> none  [per_device(): lax.all_to_all(outgoing, AXES, split_axis=0, concat_axis=0, tiled=True)]
  transfers between devices with their start and end apart: 3 -> 0, of which waited for: 3 -> 0; matrix products, arithmetic and copies ran while one was open for 3% -> 0% of each run, Pallas kernels for 0% -> 0%
where the time goes in v2:
time: 146 us
  Pallas kernels  125 us (86%)
  local copies, waits for them, and re-layouts  14.3 us (10%)
  other arithmetic  3.01 us (2%)
  matrix products  2.18 us (1%)
    pallas_call x1, Pallas kernels, run_fused(): pl.pallas_call(functools.partial(fused_kernel, n_row, n_col), in_specs=[v...  125 us
    unnamed x8, local copies, waits for them, and re-layouts  5.97 us

profile of v2, /device:TPU:0, one launch (start us, length us, event | category | flops | bytes accessed | tf_op | source)
XLA Modules:
  0.0 145.6 jit_solution(14427024688748963887)
XLA Ops:
  0.6 0.0 copy-start
  0.7 0.8 tile.4
  1.5 0.1 tile.10
  1.6 0.1 pad.12.clone
  1.6 0.7 pad_bitcast_fusion.1
  2.3 0.7 add_add_fusion.numbers_ref
  2.9 0.7 and_select_fusion
  3.6 0.2 convert_reduce_fusion.1
  3.8 0.7 multiply_add_fusion
  4.5 0.0 copy-done
  4.5 0.6 convolution_convert_fusion
  5.1 2.0 %reshape.62 = bf16[32,27648]{1,0:T(8,128)(2,1)} reshape(bf16[96,9216]{1,0:T(8,128)(2,1)S(1)} %convolution_convert_fusion) | data formatting | bytes 3538944 | tf_op jit(solution)/shard_map/reshape | solution.py:408
  7.1 1.6 %pad_bitcast_fusion = bf16[4,8,224,128]{3,1,2,0:T(8,128)(2,1)S(1)} fusion(bf16[32,27648]{1,0:T(8,128)(2,1)} %reshape.62), kind=kLoop, calls=%fused_computation.3 | loop fusion | bytes 3604480
  8.7 1.5 %copy.13 = bf16[4,8,224,128]{3,2,1,0:T(8,128)(2,1)} copy(bf16[4,8,224,128]{3,1,2,0:T(8,128)(2,1)S(1)} %pad_bitcast_fusion) | data formatting | bytes 3670016
  10.2 125.4 %shard_map.86 = (bf16[32,2048]{1,0:T(8,128)(2,1)}, bf16[32,224,128]{2,1,0:T(8,128)(2,1)}, s32[2,2,2,2,2,8,128]{6,5,4,3,2,1,0:T(8,128)}) custom-call(bf16[32,2048]{1,0:T(8,128)(2,1)} %tokens_ref.1, bf16[64,2048]{1,0:T(8,128)(2,1)} %bitcast.27, s32[8,128]{1,0:T(8,128)} %add_add_fusion.numbers_ref, bf16[32,224,128]{2,1,0:T(8,128)(2,1)} %bitcast.22, ...), custom_call_target="tpu_custom_call" | custom-call | flops 20000000000 | bytes 45000000 | tf_op jit(solution)/shard_map/pallas_call | solution.py:353
  135.6 0.9 slice.8
  136.6 0.6 convert_reduce_fusion
  137.2 0.1 select_reduce_fusion
  137.4 0.1 copy.11
  137.5 0.1 sub.28
  137.6 2.2 %copy.16 = bf16[4,8,224,128]{3,1,2,0:T(8,128)(2,1)S(1)} copy(bf16[4,8,224,128]{3,2,1,0:T(8,128)(2,1)} %bitcast.21) | data formatting | bytes 3670016
  139.8 1.3 slice.9
  141.1 2.2 %reshape.66 = bf16[96,9216]{1,0:T(8,128)(2,1)S(1)} reshape(bf16[32,27648]{1,0:T(8,128)(2,1)} %slice.9) | data formatting | bytes 3538944 | tf_op jit(solution)/shard_map/reshape | solution.py:425
  143.4 0.0 copy-start.1
  143.4 1.6 %convolution_convert_fusion.1 = bf16[72,9216]{1,0:T(8,128)(2,1)} fusion(bf16[96,9216]{1,0:T(8,128)(2,1)S(1)} %reshape.66, s32[96]{0:T(128)S(1)} %sub.28), kind=kOutput, calls=%fused_computation.1 | convolution fusion | flops 128072448 | bytes 3096960 | tf_op jit(solution)/shard_map/dot_general | solution.py:444
  144.9 0.0 copy-done.1
  144.9 0.7 copy.18
  (6 shorter events, 0.1 us)
Async XLA Ops:
  0.6 3.8 %copy-start = (bf16[72,9216]{1,0:T(8,128)(2,1)S(1)}, bf16[72,9216]{1,0:T(8,128)(2,1)}, u32[]{:S(2)}) copy-start(bf16[72,9216]{1,0:T(8,128)(2,1)} %param.12) | copy-start | bytes 3981316
  143.4 1.6 %copy-start.1 = (bf16[32,2048]{1,0:T(8,128)(2,1)S(1)}, bf16[32,2048]{1,0:T(8,128)(2,1)}, u32[]{:S(2)}) copy-start(bf16[32,2048]{1,0:T(8,128)(2,1)} %get-tuple-element.10) | copy-start | bytes 393220

commit v3 on v2

--- a/solution.py
+++ b/solution.py
@@ -130,12 +130,12 @@
 
 def fused_kernel(n_row, n_col, tokens_ref, router_ref, numbers_ref, pages_ref, w_in_hbm, w_out_hbm,
                  out_ref, arrived_ref, all_numbers_ref,
-                 x, part, gates, ranks, weighted, w_in_buf, w_out_buf, *rest):
+                 x, part, gates, ranks, weighted, activated, row_gates, w_in_buf, w_out_buf, *rest):
     devices = n_row * n_col
     dims = devices.bit_length() - 1
     row_bits = n_row.bit_length() - 1
     sends, receives = rest[:dims], rest[dims : 2 * dims]
-    (w_sem, own_sem, page_send, page_recv, gather_send, gather_recv,
+    (w_sem, v_sem, own_sem, page_send, page_recv, gather_send, gather_recv,
      sum_send, sum_recv) = rest[2 * dims :]
     row, col = lax.axis_index("row"), lax.axis_index("col")
     me = row * n_col + col
@@ -143,8 +143,8 @@
     tok_count, width = tokens_ref.shape
     halves_here, hidden, _ = w_out_hbm.shape
     rows = weighted.shape[1]
-    split = width // 2
-    columns = [pl.ds(0, split), pl.ds(split, split)]
+    split = width // 4
+    columns = [pl.ds(c * split, split) for c in range(4)]
     inner = list(range(row_bits, dims - 1))
     orders = [
         list(range(row_bits)) + inner + [dims - 1],
@@ -157,16 +157,19 @@
     def partner(b):
         return place(me + (1 - 2 * mine[b]) * 2 ** (dims - 1 - b))
 
-    def weights(j, slot):
-        return (
-            pltpu.make_async_copy(w_in_hbm.at[j], w_in_buf.at[slot], w_sem.at[slot, 0]),
-            pltpu.make_async_copy(w_out_hbm.at[j], w_out_buf.at[slot], w_sem.at[slot, 1]),
-        )
-
     slots = w_in_buf.shape[0]
-    for j in range(min(slots, halves_here)):
-        for copy in weights(j, j):
-            copy.start()
+
+    def first_weights(j):
+        slot = j % slots
+        return pltpu.make_async_copy(w_in_hbm.at[j], w_in_buf.at[slot], w_sem.at[slot])
+
+    def second_weights(j):
+        return pltpu.make_async_copy(w_out_hbm.at[j], w_out_buf.at[j], v_sem.at[j])
+
+    for j in range(slots):
+        first_weights(j).start()
+    for j in range(halves_here):
+        second_weights(j).start()
     own = pltpu.make_async_copy(pages_ref.at[me], arrived_ref.at[me], own_sem)
     own.start()
 
@@ -188,32 +191,41 @@
             device_id=place(to), device_id_type=MESH,
         )
 
-    for s in range(dims):
+    def gather(g, s):
         copies = []
-        for h in range(3):
+        for h in range(3 - g):
             order = orders[h % 2]
             done, b = order[:s], order[s]
             index = tuple(slice(None) if d in done else mine[d] for d in range(dims))
             if h < 2:
-                ref = x.at[index + (slice(None), columns[h])]
+                ref = x.at[index + (slice(None), columns[2 * g + h])]
             else:
                 ref = all_numbers_ref.at[index]
             copies.append(
                 pltpu.make_async_remote_copy(
                     src_ref=ref, dst_ref=ref,
-                    send_sem=gather_send.at[s, h], recv_sem=gather_recv.at[s, h],
+                    send_sem=gather_send.at[s, 2 * h + g], recv_sem=gather_recv.at[s, 2 * h + g],
                     device_id=partner(b), device_id_type=MESH,
                 )
             )
-        for copy in copies:
-            copy.start()
-        for copy in copies:
-            copy.wait()
-        if s == row_bits - 1:
-
-            @pl.loop(1, devices)
-            def _(o):
-                page(o).start()
+        return copies
+
+    for tick in range(dims + 1):
+        for g in range(2):
+            s = tick - g
+            if 0 < s <= dims:
+                for copy in gather(g, s - 1):
+                    copy.wait()
+            if 0 <= s < dims:
+                for copy in gather(g, s):
+                    copy.start()
+
+    @pl.loop(1, devices)
+    def _(o):
+        page(o).start()
+
+    for copy in gather(1, dims - 1):
+        copy.wait()
 
     chunk = devices // 2 * tok_count
     group = 128 // tok_count
@@ -259,7 +271,6 @@
 
     @pl.loop(0, halves_here)
     def _(j):
-        slot = j % slots
         expert = base + j
         picked_rows = jnp.zeros((rows, width), jnp.float32)
         row_gate = jnp.zeros((rows, 1), jnp.float32)
@@ -273,34 +284,44 @@
                 jnp.where(hit, gates[pl.ds(expert, 1), q * chunk : (q + 1) * chunk], 0.0),
                 axis=1, keepdims=True,
             )
-        w_first, w_second = weights(j, slot)
-        w_first.wait()
+        row_gates[pl.ds(j, 1)] = row_gate[None]
+        first_weights(j).wait()
         gate_up = jnp.dot(
-            picked_rows.astype(jnp.bfloat16), w_in_buf[slot], preferred_element_type=jnp.float32
+            picked_rows.astype(jnp.bfloat16), w_in_buf[j % slots],
+            preferred_element_type=jnp.float32,
         )
         gate = gate_up[:, :hidden]
-        activated = (gate / (1.0 + jnp.exp(-gate)) * gate_up[:, hidden:]).astype(jnp.bfloat16)
-        w_second.wait()
-        half = jnp.dot(activated, w_out_buf[slot], preferred_element_type=jnp.float32)
-        weighted[pl.ds(j, 1)] = (half * row_gate).astype(jnp.bfloat16)[None]
+        activated[pl.ds(j, 1)] = (
+            gate / (1.0 + jnp.exp(-gate)) * gate_up[:, hidden:]
+        ).astype(jnp.bfloat16)[None]
 
         @pl.when(j + slots < halves_here)
         def _():
-            for copy in weights(j + slots, slot):
-                copy.start()
-
-    for q in range(2):
-        hits = jnp.concatenate(
-            [
-                chosen(base + j, q).astype(jnp.float32).astype(jnp.bfloat16)
-                for j in range(halves_here)
-            ],
-            axis=0,
-        )
-        part[pl.ds(q * (devices // 2), devices // 2)] = lax.dot_general(
-            hits, weighted[...].reshape(halves_here * rows, width),
-            (((0,), (0,)), ((), ())), preferred_element_type=jnp.float32,
-        ).reshape(devices // 2, tok_count, width)
+            first_weights(j + slots).start()
+
+    for j in range(halves_here):
+        second_weights(j).wait()
+
+    def sum_experts(g):
+        begin, size = 2 * g * split, 2 * split
+        for j in range(halves_here):
+            half = jnp.dot(
+                activated[j], w_out_buf[j, :, begin : begin + size],
+                preferred_element_type=jnp.float32,
+            )
+            weighted[j, :, begin : begin + size] = (half * row_gates[j]).astype(jnp.bfloat16)
+        for q in range(2):
+            hits = jnp.concatenate(
+                [
+                    chosen(base + j, q).astype(jnp.float32).astype(jnp.bfloat16)
+                    for j in range(halves_here)
+                ],
+                axis=0,
+            )
+            part[pl.ds(q * (devices // 2), devices // 2), :, pl.ds(begin, size)] = lax.dot_general(
+                hits, weighted[:, :, begin : begin + size].reshape(halves_here * rows, size),
+                (((0,), (0,)), ((), ())), preferred_element_type=jnp.float32,
+            ).reshape(devices // 2, tok_count, size)
 
     def blocks(order, s, flip):
         fixed = {b: mine[b] for b in order[:s]}
@@ -312,23 +333,38 @@
                 bits[d] = (i >> (len(free) - 1 - place_of)) & 1
             yield i, sum(bits[d] * 2 ** (dims - 1 - d) for d in range(dims))
 
-    for s in range(dims):
-        copies = []
+    def sum_copy(g, s, h):
+        cols = columns[2 * g + h]
+        return pltpu.make_async_remote_copy(
+            src_ref=sends[s].at[:, :, cols], dst_ref=receives[s].at[:, :, cols],
+            send_sem=sum_send.at[s, 2 * h + g], recv_sem=sum_recv.at[s, 2 * h + g],
+            device_id=partner(orders[h][dims - 1 - s]), device_id_type=MESH,
+        )
+
+    def sum_start(g, s):
         for h in range(2):
-            order = orders[h][::-1]
-            for i, block in blocks(order, s, True):
-                sends[s][i, :, columns[h]] = part[block, :, columns[h]].astype(jnp.bfloat16)
-            copy = pltpu.make_async_remote_copy(
-                src_ref=sends[s].at[:, :, columns[h]], dst_ref=receives[s].at[:, :, columns[h]],
-                send_sem=sum_send.at[s, h], recv_sem=sum_recv.at[s, h],
-                device_id=partner(order[s]), device_id_type=MESH,
-            )
-            copy.start()
-            copies.append(copy)
+            cols = columns[2 * g + h]
+            for i, block in blocks(orders[h][::-1], s, True):
+                sends[s][i, :, cols] = part[block, :, cols].astype(jnp.bfloat16)
+            sum_copy(g, s, h).start()
+
+    def sum_finish(g, s):
         for h in range(2):
-            copies[h].wait()
+            cols = columns[2 * g + h]
+            sum_copy(g, s, h).wait()
             for i, block in blocks(orders[h][::-1], s, False):
-                part[block, :, columns[h]] += receives[s][i, :, columns[h]].astype(jnp.float32)
+                part[block, :, cols] += receives[s][i, :, cols].astype(jnp.float32)
+
+    sum_experts(0)
+    sum_start(0, 0)
+    sum_experts(1)
+    for tick in range(1, dims + 2):
+        for g in range(2):
+            s = tick - g
+            if 0 < s <= dims:
+                sum_finish(g, s - 1)
+            if 0 <= s < dims:
+                sum_start(g, s)
     out_ref[...] = part[me].astype(jnp.bfloat16)
 
     own.wait()
@@ -346,7 +382,7 @@
     count = devices * tok_count
     rows = CAPE * devices
     cube = (2,) * dims
-    slots = min(2, halves_here)
+    slots = min(3, halves_here)
     vmem = pl.BlockSpec(memory_space=pltpu.VMEM)
     anywhere = pl.BlockSpec(memory_space=pl.ANY)
     parts = [pltpu.VMEM((2 ** (dims - 1 - s), tok_count, width), jnp.bfloat16) for s in range(dims)]
@@ -365,18 +401,21 @@
             pltpu.VMEM((EXPERTS, count), jnp.float32),
             pltpu.VMEM((EXPERTS, count), jnp.float32),
             pltpu.VMEM((halves_here, rows, width), jnp.bfloat16),
+            pltpu.VMEM((halves_here, rows, hidden), jnp.bfloat16),
+            pltpu.VMEM((halves_here, rows, 1), jnp.float32),
             pltpu.VMEM((slots,) + w_in.shape[1:], jnp.bfloat16),
-            pltpu.VMEM((slots,) + w_out.shape[1:], jnp.bfloat16),
+            pltpu.VMEM(w_out.shape, jnp.bfloat16),
             *parts,
             *parts,
-            pltpu.SemaphoreType.DMA((slots, 2)),
+            pltpu.SemaphoreType.DMA((slots,)),
+            pltpu.SemaphoreType.DMA((halves_here,)),
             pltpu.SemaphoreType.DMA(()),
             pltpu.SemaphoreType.DMA((devices,)),
             pltpu.SemaphoreType.DMA((devices,)),
-            pltpu.SemaphoreType.DMA((dims, 3)),
-            pltpu.SemaphoreType.DMA((dims, 3)),
-            pltpu.SemaphoreType.DMA((dims, 2)),
-            pltpu.SemaphoreType.DMA((dims, 2)),
+            pltpu.SemaphoreType.DMA((dims, 6)),
+            pltpu.SemaphoreType.DMA((dims, 6)),
+            pltpu.SemaphoreType.DMA((dims, 4)),
+            pltpu.SemaphoreType.DMA((dims, 4)),
         ],
         compiler_params=pltpu.CompilerParams(
             collective_id=0, has_side_effects=True, vmem_limit_bytes=60 << 20
@@ -387,6 +426,113 @@
     )(tokens, router_t, numbers, pages, w_in, w_out)
 
 
+def page_places(rows, page_cap):
+    row = lax.broadcasted_iota(jnp.int32, (rows, 128), 0)
+    within = lax.rem(row, 16)
+    return lax.div(row, 16), lax.div(within, page_cap), lax.rem(within, page_cap)
+
+
+def pack_kernel(page_cap, pages_here, slot_ref, routes_ref, cache_ref, pages_ref, numbers_ref,
+                slot_row, stacked):
+    me = lax.axis_index("row") * lax.axis_size("col") + lax.axis_index("col")
+    rows, part_width = pages_ref.shape
+    parts = 16 // page_cap
+    page_width = cache_ref.shape[1]
+    top_count, tok_count = routes_ref.shape
+    numbers_ref[...] = jnp.zeros_like(numbers_ref)
+    group = 128 // tok_count
+    for i in range(group):
+        numbers_ref[:top_count, i * tok_count : (i + 1) * tok_count] = jnp.where(
+            me % group == i, routes_ref[...], 0
+        )
+    numbers_ref[top_count : top_count + 1, :pages_here] = slot_ref[...]
+    slot_row[...] = jnp.zeros_like(slot_row)
+    slot_row[:, :pages_here] = slot_ref[...]
+    target = lax.div(slot_row[...], pages_here)
+    across = jnp.broadcast_to(target.astype(jnp.float32), (128, 128))
+    upper = lax.broadcasted_iota(jnp.int32, (128, 128), 0) < lax.broadcasted_iota(
+        jnp.int32, (128, 128), 1
+    )
+    same = (across.T == across) & upper
+    rank = jnp.sum(jnp.where(same, 1.0, 0.0), axis=0, keepdims=True).astype(jnp.int32)
+    live = lax.broadcasted_iota(jnp.int32, (1, 128), 1) < pages_here
+    placed = jnp.where(live, target * page_cap + rank, -1)
+    dest, part_of, nth = page_places(rows, page_cap)
+    match = (dest * page_cap + nth) == placed
+    stacked[...] = jnp.zeros_like(stacked)
+    picks = []
+    for p in range(parts):
+        size = min(part_width, page_width - p * part_width)
+        stacked[p * 128 : p * 128 + pages_here, :size] = cache_ref[
+            :, p * part_width : p * part_width + size
+        ]
+        picks.append(jnp.where(match & (part_of == p), 1.0, 0.0).astype(jnp.bfloat16))
+    pages_ref[...] = jnp.dot(
+        jnp.concatenate(picks, axis=1), stacked[...], preferred_element_type=jnp.float32
+    ).astype(jnp.bfloat16)
+
+
+def place_kernel(page_cap, top_count, numbers_ref, arrived_ref, out_ref):
+    me = lax.axis_index("row") * lax.axis_size("col") + lax.axis_index("col")
+    rows, part_width = arrived_ref.shape
+    pages_here, page_width = out_ref.shape
+    slots = numbers_ref[:, top_count, :]
+    slots = jnp.broadcast_to(slots[:, None, :], (rows // 16, 16, 128)).reshape(rows, 128)
+    lane = lax.broadcasted_iota(jnp.int32, (rows, 128), 1)
+    mine = (lax.div(slots, pages_here) == me) & (lane < pages_here)
+    earlier = lax.broadcasted_iota(jnp.int32, (128, 128), 0) < lax.broadcasted_iota(
+        jnp.int32, (128, 128), 1
+    )
+    rank = jnp.dot(
+        jnp.where(mine, 1.0, 0.0).astype(jnp.bfloat16),
+        jnp.where(earlier, 1.0, 0.0).astype(jnp.bfloat16),
+        preferred_element_type=jnp.float32,
+    )
+    _, part_of, nth = page_places(rows, page_cap)
+    taken = mine & (rank == nth.astype(jnp.float32))
+    within = lax.rem(slots, pages_here).astype(jnp.float32) + 1.0
+    landing = jnp.sum(jnp.where(taken, within, 0.0), axis=1, keepdims=True) - 1.0
+    match = landing == lane.astype(jnp.float32)
+    for p in range(16 // page_cap):
+        size = min(part_width, page_width - p * part_width)
+        pick = jnp.where(match & (part_of == p), 1.0, 0.0).astype(jnp.bfloat16)
+        out_ref[:, p * part_width : p * part_width + size] = lax.dot_general(
+            pick, arrived_ref[:, :size], (((0,), (0,)), ((), ())),
+            preferred_element_type=jnp.float32,
+        )[:pages_here].astype(jnp.bfloat16)
+
+
+def pack_pages(page_slot, routes, cache_prefill, devices, page_cap):
+    pages_here, page_width = cache_prefill.shape
+    parts = 16 // page_cap
+    part_width = -(-page_width // (parts * 128)) * 128
+    rows = devices * 16
+    return pl.pallas_call(
+        functools.partial(pack_kernel, page_cap, pages_here),
+        in_specs=[pl.BlockSpec(memory_space=pltpu.VMEM)] * 3,
+        out_specs=[pl.BlockSpec(memory_space=pltpu.VMEM)] * 2,
+        out_shape=[
+            jax.ShapeDtypeStruct((rows, part_width), jnp.bfloat16),
+            jax.ShapeDtypeStruct((8, 128), jnp.int32),
+        ],
+        scratch_shapes=[
+            pltpu.VMEM((1, 128), jnp.int32),
+            pltpu.VMEM((parts * 128, part_width), jnp.bfloat16),
+        ],
+        compiler_params=pltpu.CompilerParams(vmem_limit_bytes=48 << 20),
+    )(page_slot[None], routes.T, cache_prefill)
+
+
+def place_pages(numbers, arrived, shape, page_cap, top_count):
+    return pl.pallas_call(
+        functools.partial(place_kernel, page_cap, top_count),
+        in_specs=[pl.BlockSpec(memory_space=pltpu.VMEM)] * 2,
+        out_specs=pl.BlockSpec(memory_space=pltpu.VMEM),
+        out_shape=jax.ShapeDtypeStruct(shape, jnp.bfloat16),
+        compiler_params=pltpu.CompilerParams(vmem_limit_bytes=48 << 20),
+    )(numbers, arrived)
+
+
 def per_device(tokens, routes, router, w_in, w_out, cache_prefill, page_slot):
     devices = lax.axis_size(AXES)
     me = lax.axis_index(AXES)
@@ -395,6 +541,18 @@
     tok_count, top_count = routes.shape
     halves_here = w_in.shape[0]
 
+    if devices * tok_count <= FUSED_TOKENS and tok_count * 4 <= 128 and pages_here <= 128:
+        pages, block = pack_pages(page_slot, routes, cache_prefill, devices, page_cap)
+        moe_out, arrived, numbers = run_fused(
+            lax.axis_size("row"), lax.axis_size("col"), tokens, router.T, block,
+            pages.reshape(devices, 16, -1), w_in, w_out,
+        )
+        cache_decode = place_pages(
+            numbers.reshape(devices, 8, 128), arrived.reshape(pages.shape),
+            cache_prefill.shape, page_cap, top_count,
+        )
+        return moe_out, cache_decode
+
     target = page_slot // pages_here
     same = target[:, None] == target[None, :]
     earlier = jnp.arange(pages_here)[None, :] < jnp.arange(pages_here)[:, None]
@@ -403,38 +561,16 @@
     outgoing = jnp.dot(send_pick, cache_prefill, preferred_element_type=jnp.float32).astype(
         jnp.bfloat16
     )
-    if devices * tok_count <= FUSED_TOKENS and tok_count * 4 <= 128:
-        pad = -(page_cap * page_width) % (16 * 128)
-        pages = outgoing.reshape(devices, page_cap * page_width)
-        pages = jnp.pad(pages, ((0, 0), (0, pad))).reshape(devices, -1, 128)
-        lane = jnp.arange(128) // tok_count
-        spread = jnp.tile(routes.T, (1, 128 // tok_count))
-        spread = jnp.where(lane[None, :] == me % (128 // tok_count), spread, 0)
-        block = jnp.concatenate(
-            [
-                spread,
-                jnp.pad(page_slot, (0, 128 - pages_here))[None],
-                jnp.zeros((7 - top_count, 128), jnp.int32),
-            ],
-            axis=0,
-        )
-        moe_out, arrived, numbers = run_fused(
-            lax.axis_size("row"), lax.axis_size("col"), tokens, router.T, block, pages, w_in, w_out
-        )
-        arrived = arrived.reshape(devices, -1)[:, : page_cap * page_width]
-        arrived = arrived.reshape(devices * page_cap, page_width)
-        slots = numbers.reshape(devices, 8, 128)[:, top_count, :pages_here]
-    else:
-        arrived = lax.all_to_all(outgoing, AXES, split_axis=0, concat_axis=0, tiled=True)
-
-        numbers = jnp.concatenate([routes.reshape(-1), page_slot])
-        numbers = lax.all_gather(numbers[None], AXES, axis=0, tiled=True)
-        x = lax.all_gather(tokens, AXES, axis=0, tiled=True)
-        all_routes = numbers[:, : tok_count * top_count].reshape(devices * tok_count, top_count)
-        base = jnp.reshape((me * halves_here) % EXPERTS, (1,)).astype(jnp.int32)
-        partial = run_experts(base, x, router.T, all_routes.T, w_in, w_out, devices)
-        moe_out = lax.psum_scatter(partial, AXES, scatter_dimension=0, tiled=True)
-        slots = numbers[:, tok_count * top_count :]
+    arrived = lax.all_to_all(outgoing, AXES, split_axis=0, concat_axis=0, tiled=True)
+
+    numbers = jnp.concatenate([routes.reshape(-1), page_slot])
+    numbers = lax.all_gather(numbers[None], AXES, axis=0, tiled=True)
+    x = lax.all_gather(tokens, AXES, axis=0, tiled=True)
+    all_routes = numbers[:, : tok_count * top_count].reshape(devices * tok_count, top_count)
+    base = jnp.reshape((me * halves_here) % EXPERTS, (1,)).astype(jnp.int32)
+    partial = run_experts(base, x, router.T, all_routes.T, w_in, w_out, devices)
+    moe_out = lax.psum_scatter(partial, AXES, scatter_dimension=0, tiled=True)
+    slots = numbers[:, tok_count * top_count :]
 
     mine = slots // pages_here == me
     order = jnp.sum((mine[:, None, :] & earlier[None]).astype(jnp.int32), axis=2)

time: 146 us -> 115 us (0.79)
  Pallas kernels: 125 us -> 107 us
  local copies, waits for them, and re-layouts: 14.3 us -> 7.64 us
  other arithmetic: 3.01 us -> 0 us
  matrix products: 2.18 us -> 0 us
    pallas_call x1, Pallas kernels: 125 us -> 102 us  [run_fused(): pl.pallas_call(functools.partial(fused_kernel, n_row, n_col), in_specs=[v...]
    pallas_call x0 -> x2, Pallas kernels: none -> 4.75 us  [the longest x1 2.83 us: place_pages(): pl.pallas_call(functools.partial(place_kernel, page_cap, top_count), in_s...]
    reshape x2 -> x0, local copies, waits for them, and re-layouts: 4.25 us -> none  [the longest x1 2.23 us: per_device(): arrived = arrived.reshape(devices * page_cap, page_width)]
    slice x2 -> x0, local copies, waits for them, and re-layouts: 2.25 us -> none  [the longest x1 1.33 us: per_device(): arrived = arrived.reshape(devices, -1)[:, :page_cap * page_width]]
    dot_general x2 -> x0, matrix products: 2.18 us -> none  [the longest x1 1.56 us: per_device(): jnp.dot(land_pick, arrived, preferred_element_type=jnp.float32)]
    unnamed x8 -> x17, local copies, waits for them, and re-layouts: 5.97 us -> 7.64 us
where the time goes in v3:
time: 115 us
  Pallas kernels  107 us (93%)
  local copies, waits for them, and re-layouts  7.64 us (7%)
    pallas_call x1, Pallas kernels, run_fused(): pl.pallas_call(functools.partial(fused_kernel, n_row, n_col), in_specs=[v...  102 us
    unnamed x17, local copies, waits for them, and re-layouts  7.64 us
    pallas_call x1, Pallas kernels, place_pages(): pl.pallas_call(functools.partial(place_kernel, page_cap, top_count), in_s...  2.83 us

profile of v3, /device:TPU:0, one launch (start us, length us, event | category | flops | bytes accessed | tf_op | source)
XLA Modules:
  0.0 114.9 jit_solution(2317839380902312322)
XLA Ops:
  0.6 0.0 copy-start.1
  0.6 1.3 %copy-done.1 = bf16[72,9216]{1,0:T(8,128)(2,1)S(1)} copy-done((bf16[72,9216]{1,0:T(8,128)(2,1)S(1)}, bf16[72,9216]{1,0:T(8,128)(2,1)}, u32[]{:S(2)}) %copy-start.1) | copy-done | bytes 1327128
  2.0 0.0 copy-start.3
  2.0 0.7 copy-done.3
  2.6 0.0 copy-start.4
  2.6 0.7 copy-done.4
  3.3 1.9 %shard_map.86 = (bf16[512,1920]{1,0:T(8,128)(2,1)S(1)}, s32[8,128]{1,0:T(8,128)S(1)}) custom-call(s32[1,72]{1,0:T(1,128)S(1)} %bitcast.9, s32[6,32]{1,0:T(8,128)S(1)} %bitcast.8, bf16[72,9216]{1,0:T(8,128)(2,1)S(1)} %copy-done.1), custom_call_target="tpu_custom_call" | custom-call | tf_op jit(solution)/shard_map/pallas_call | solution.py:510
  5.2 0.0 copy-start.5
  5.2 1.3 %copy-done.5 = bf16[512,1920]{1,0:T(8,128)(2,1)} copy-done((bf16[512,1920]{1,0:T(8,128)(2,1)}, bf16[512,1920]{1,0:T(8,128)(2,1)S(1)}, u32[]{:S(2)}) %copy-start.5) | copy-done | bytes 1966104
  6.5 0.0 copy-start.6
  6.5 0.6 copy-done.6
  7.1 101.8 %shard_map.87 = (bf16[32,2048]{1,0:T(8,128)(2,1)}, bf16[32,16,1920]{2,1,0:T(8,128)(2,1)}, s32[2,2,2,2,2,8,128]{6,5,4,3,2,1,0:T(8,128)}) custom-call(bf16[32,2048]{1,0:T(8,128)(2,1)} %tokens_ref.1, bf16[64,2048]{1,0:T(8,128)(2,1)} %bitcast.11, s32[8,128]{1,0:T(8,128)} %copy-done.6, bf16[32,16,1920]{2,1,0:T(8,128)(2,1)} %bitcast.10, ...), custom_call_target="tpu_custom_call" | custom-call | flops 20000000000 | bytes 45000000 | tf_op jit(solution)/shard_map/pallas_call | solution.py:389
  108.9 0.0 copy-start
  108.9 1.5 %copy-done = bf16[32,16,1920]{2,1,0:T(8,128)(2,1)S(1)} copy-done((bf16[32,16,1920]{2,1,0:T(8,128)(2,1)S(1)}, bf16[32,16,1920]{2,1,0:T(8,128)(2,1)}, u32[]{:S(2)}) %copy-start) | copy-done | bytes 1966104
  110.5 0.0 copy-start.2
  110.5 0.9 copy-done.2
  111.4 0.0 copy-start.7
  111.4 2.8 %shard_map.88 = bf16[72,9216]{1,0:T(8,128)(2,1)} custom-call(s32[32,8,128]{2,1,0:T(8,128)S(1)} %bitcast.7, bf16[512,1920]{1,0:T(8,128)(2,1)S(1)} %bitcast.6), custom_call_target="tpu_custom_call" | custom-call | tf_op jit(solution)/shard_map/pallas_call | solution.py:527
  114.2 0.0 copy-done.7
  114.2 0.7 copy.10
Async XLA Ops:
  0.6 1.3 %copy-start.1 = (bf16[72,9216]{1,0:T(8,128)(2,1)S(1)}, bf16[72,9216]{1,0:T(8,128)(2,1)}, u32[]{:S(2)}) copy-start(bf16[72,9216]{1,0:T(8,128)(2,1)} %cache_ref.1) | copy-start | bytes 3981316
  2.0 0.7 copy-start.3
  2.6 0.7 copy-start.4
  5.2 1.3 %copy-start.5 = (bf16[512,1920]{1,0:T(8,128)(2,1)}, bf16[512,1920]{1,0:T(8,128)(2,1)S(1)}, u32[]{:S(2)}) copy-start(bf16[512,1920]{1,0:T(8,128)(2,1)S(1)} %get-tuple-element.8) | copy-start | bytes 5898244
  6.5 0.6 copy-start.6
  108.9 1.5 %copy-start = (bf16[32,16,1920]{2,1,0:T(8,128)(2,1)S(1)}, bf16[32,16,1920]{2,1,0:T(8,128)(2,1)}, u32[]{:S(2)}) copy-start(bf16[32,16,1920]{2,1,0:T(8,128)(2,1)} %get-tuple-element.11) | copy-start | bytes 5898244
  110.5 0.9 copy-start.2
  111.4 2.8 %copy-start.7 = (bf16[32,2048]{1,0:T(8,128)(2,1)S(1)}, bf16[32,2048]{1,0:T(8,128)(2,1)}, u32[]{:S(2)}) copy-start(bf16[32,2048]{1,0:T(8,128)(2,1)} %get-tuple-element.14) | copy-start | bytes 393220

commit v4 on v3

--- a/solution.py
+++ b/solution.py
@@ -191,6 +191,9 @@
             device_id=place(to), device_id_type=MESH,
         )
 
+    def start_page(to_row, to_col):
+        page((to_row * n_col + to_col - me + devices) % devices).start()
+
     def gather(g, s):
         copies = []
         for h in range(3 - g):
@@ -219,10 +222,24 @@
             if 0 <= s < dims:
                 for copy in gather(g, s):
                     copy.start()
-
-    @pl.loop(1, devices)
-    def _(o):
-        page(o).start()
+        if tick == 0:
+
+            @pl.loop(1, n_col)
+            def _(i):
+                start_page(row, (col + i) % n_col)
+
+        if tick == row_bits:
+
+            @pl.loop(0, 2 * (n_row - 1))
+            def _(i):
+                start_page((row + 1 + i // 2) % n_row, col // 2 * 2 + i % 2)
+
+    @pl.loop(0, (n_row - 1) * (n_col - 2))
+    def _(i):
+        start_page(
+            (row + 1 + i % (n_row - 1)) % n_row,
+            (col // 2 * 2 + 2 + i // (n_row - 1)) % n_col,
+        )
 
     for copy in gather(1, dims - 1):
         copy.wait()

time: 115 us -> 113 us (0.983)
  Pallas kernels: 107 us -> 104 us
    pallas_call x1, Pallas kernels: 102 us -> 99.4 us  [run_fused(): pl.pallas_call(functools.partial(fused_kernel, n_row, n_col), in_specs=[v...]
where the time goes in v4:
time: 113 us; the launch traced here: 112 us
  Pallas kernels  104 us (92%)
  local copies, waits for them, and re-layouts  7.64 us (7%)
    pallas_call x1, Pallas kernels, run_fused(): pl.pallas_call(functools.partial(fused_kernel, n_row, n_col), in_specs=[v...  99.4 us
    unnamed x17, local copies, waits for them, and re-layouts  7.64 us
    pallas_call x1, Pallas kernels, place_pages(): pl.pallas_call(functools.partial(place_kernel, page_cap, top_count), in_s...  2.83 us

profile of v4, /device:TPU:0, one launch (start us, length us, event | category | flops | bytes accessed | tf_op | source)
XLA Modules:
  0.0 112.5 jit_solution(949059323898929493)
XLA Ops:
  0.6 0.0 copy-start.1
  0.6 1.3 %copy-done.1 = bf16[72,9216]{1,0:T(8,128)(2,1)S(1)} copy-done((bf16[72,9216]{1,0:T(8,128)(2,1)S(1)}, bf16[72,9216]{1,0:T(8,128)(2,1)}, u32[]{:S(2)}) %copy-start.1) | copy-done | bytes 1327128
  2.0 0.0 copy-start.3
  2.0 0.7 copy-done.3
  2.6 0.0 copy-start.4
  2.6 0.7 copy-done.4
  3.3 1.9 %shard_map.86 = (bf16[512,1920]{1,0:T(8,128)(2,1)S(1)}, s32[8,128]{1,0:T(8,128)S(1)}) custom-call(s32[1,72]{1,0:T(1,128)S(1)} %bitcast.9, s32[6,32]{1,0:T(8,128)S(1)} %bitcast.8, bf16[72,9216]{1,0:T(8,128)(2,1)S(1)} %copy-done.1), custom_call_target="tpu_custom_call" | custom-call | tf_op jit(solution)/shard_map/pallas_call | solution.py:527
  5.2 0.0 copy-start.5
  5.2 1.3 %copy-done.5 = bf16[512,1920]{1,0:T(8,128)(2,1)} copy-done((bf16[512,1920]{1,0:T(8,128)(2,1)}, bf16[512,1920]{1,0:T(8,128)(2,1)S(1)}, u32[]{:S(2)}) %copy-start.5) | copy-done | bytes 1966104
  6.5 0.0 copy-start.6
  6.5 0.6 copy-done.6
  7.1 99.4 %shard_map.87 = (bf16[32,2048]{1,0:T(8,128)(2,1)}, bf16[32,16,1920]{2,1,0:T(8,128)(2,1)}, s32[2,2,2,2,2,8,128]{6,5,4,3,2,1,0:T(8,128)}) custom-call(bf16[32,2048]{1,0:T(8,128)(2,1)} %tokens_ref.1, bf16[64,2048]{1,0:T(8,128)(2,1)} %bitcast.11, s32[8,128]{1,0:T(8,128)} %copy-done.6, bf16[32,16,1920]{2,1,0:T(8,128)(2,1)} %bitcast.10, ...), custom_call_target="tpu_custom_call" | custom-call | flops 20000000000 | bytes 45000000 | tf_op jit(solution)/shard_map/pallas_call | solution.py:406
  106.5 0.0 copy-start
  106.5 1.5 %copy-done = bf16[32,16,1920]{2,1,0:T(8,128)(2,1)S(1)} copy-done((bf16[32,16,1920]{2,1,0:T(8,128)(2,1)S(1)}, bf16[32,16,1920]{2,1,0:T(8,128)(2,1)}, u32[]{:S(2)}) %copy-start) | copy-done | bytes 1966104
  108.1 0.0 copy-start.2
  108.1 0.9 copy-done.2
  109.0 0.0 copy-start.7
  109.0 2.8 %shard_map.88 = bf16[72,9216]{1,0:T(8,128)(2,1)} custom-call(s32[32,8,128]{2,1,0:T(8,128)S(1)} %bitcast.7, bf16[512,1920]{1,0:T(8,128)(2,1)S(1)} %bitcast.6), custom_call_target="tpu_custom_call" | custom-call | tf_op jit(solution)/shard_map/pallas_call | solution.py:544
  111.8 0.0 copy-done.7
  111.8 0.7 copy.10
Async XLA Ops:
  0.6 1.3 %copy-start.1 = (bf16[72,9216]{1,0:T(8,128)(2,1)S(1)}, bf16[72,9216]{1,0:T(8,128)(2,1)}, u32[]{:S(2)}) copy-start(bf16[72,9216]{1,0:T(8,128)(2,1)} %cache_ref.1) | copy-start | bytes 3981316
  2.0 0.7 copy-start.3
  2.6 0.7 copy-start.4
  5.2 1.3 %copy-start.5 = (bf16[512,1920]{1,0:T(8,128)(2,1)}, bf16[512,1920]{1,0:T(8,128)(2,1)S(1)}, u32[]{:S(2)}) copy-start(bf16[512,1920]{1,0:T(8,128)(2,1)S(1)} %get-tuple-element.8) | copy-start | bytes 5898244
  6.5 0.6 copy-start.6
  106.5 1.5 %copy-start = (bf16[32,16,1920]{2,1,0:T(8,128)(2,1)S(1)}, bf16[32,16,1920]{2,1,0:T(8,128)(2,1)}, u32[]{:S(2)}) copy-start(bf16[32,16,1920]{2,1,0:T(8,128)(2,1)} %get-tuple-element.11) | copy-start | bytes 5898244
  108.1 0.9 copy-start.2
  109.0 2.8 %copy-start.7 = (bf16[32,2048]{1,0:T(8,128)(2,1)S(1)}, bf16[32,2048]{1,0:T(8,128)(2,1)}, u32[]{:S(2)}) copy-start(bf16[32,2048]{1,0:T(8,128)(2,1)} %get-tuple-element.14) | copy-start | bytes 393220
